TPU v7x, 256 devices: a whole 4x4x8 slice. The times are simulated.
256 devices in a mesh: ctx: 64 (over z, y_lo, x), tp: 4 (over y_hi, core).
Axes of the slice: x: 4, y: 4 (y_hi: 2, y_lo: 2; y = y_hi * 2 + y_lo), z: 8, core: 2. Of those that a mesh axis runs over, the one named last changes fastest.
Arguments:
- queries: bfloat16 [8192, 6144], P('ctx', 'tp'), may hold values from -5 to 5
- keys_values: bfloat16 [8192, 2, 8, 128], P(('ctx', 'tp')), may hold values from -5 to 5
- segment_ids: int32 [8192], P('ctx'), may hold values from 0 to 3, never falling along the last dimension, each value on 1 to 6144 neighbouring positions
Outputs:
- attended: bfloat16 [8192, 6144], P('ctx', 'tp')
- log_sums: float32 [48, 8192], P('tp', 'ctx')
Inputs may be any that keep to these rules, and one draw needn't show every extreme that they name: `segment_ids`: never falls along the tokens; every document has 1 to 6144 tokens, and one has exactly 6144.
All inputs are finite; a program needn't handle non-finite values.
Results may differ from a plain program's by a relative error of at most 0.0055.
Values may be sent and summed in bfloat16 or wider, within the bound.
A program may use at most 192 MiB of HBM per device.

v0:
```python
import jax
import jax.numpy as jnp
from jax import lax
from jax.sharding import PartitionSpec as P

Q_HEADS = 48
KV_HEADS = 8
HEAD = 128


def shards(queries, keys_values, segment_ids):
    my_index = lax.axis_index("ctx")
    rows = queries.shape[0]
    group = Q_HEADS // KV_HEADS
    factor = HEAD ** (-0.5)
    local_kv = lax.all_to_all(keys_values, "tp", split_axis=2, concat_axis=0, tiled=True)
    kv_local = local_kv.shape[2]
    own_block = local_kv.reshape(rows, 2 * kv_local * HEAD)
    all_segments = lax.all_gather(segment_ids, "ctx", axis=0, tiled=True)
    query_heads = queries.reshape(rows, kv_local, group, HEAD)
    query_pos = my_index * rows + jnp.arange(rows, dtype=jnp.int32)

    def update(state, pieces, allowed):
        running, total, accum = state
        keys = pieces[:, 0]
        values = pieces[:, 1]
        scores = (
            jnp.einsum("qhgd,khd->hgqk", query_heads, keys, preferred_element_type=jnp.float32)
            * factor
        )
        scores = jnp.where(allowed[None, None], scores, jnp.float32(-1e30))
        new_max = jnp.maximum(running, jnp.max(scores, axis=-1))
        weights = jnp.where(
            allowed[None, None], jnp.exp(scores - new_max[..., None]), jnp.float32(0.0)
        )
        total = jnp.sum(weights, axis=-1)
        rounded = weights.astype(jnp.bfloat16)
        accum = jnp.einsum("hgqk,khd->hgqd", rounded, values, preferred_element_type=jnp.float32)
        return (new_max, total, accum)

    state = (
        jnp.full((kv_local, group, rows), -1e30, jnp.float32),
        jnp.zeros((kv_local, group, rows), jnp.float32),
        jnp.zeros((kv_local, group, rows, HEAD), jnp.float32),
    )
    piece = lax.all_gather(own_block, "ctx", axis=0, tiled=True)
    count = piece.shape[0]
    pieces = piece.reshape(count, 2, kv_local, HEAD)
    key_pos = jnp.arange(count, dtype=jnp.int32)
    allowed = (key_pos[None, :] <= query_pos[:, None]) & (
        all_segments[None, :] == segment_ids[:, None]
    )
    state = lax.cond(
        jnp.any(allowed), lambda inner: update(inner, pieces, allowed), lambda inner: inner, state
    )
    running, total, accum = state
    output = (accum / total[..., None]).astype(jnp.bfloat16)
    attended = jnp.transpose(output, (2, 0, 1, 3)).reshape(rows, kv_local * group * HEAD)
    log_sums = (running + jnp.log(total)).reshape(kv_local * group, rows)
    return (attended, log_sums)


def solution(mesh):
    placed = (P("ctx", "tp"), P(("ctx", "tp"), None, None, None), P("ctx"))
    return jax.shard_map(
        shards,
        mesh=mesh,
        in_specs=placed,
        out_specs=(P("ctx", "tp"), P("tp", "ctx")),
        check_vma=False,
    )
```

profile of v0, /device:TPU:16, one launch (start us, length us, event | category | flops | bytes accessed | tf_op | source)
XLA Modules:
  0.0 419.7 jit_solution(1726629303250437791)
XLA Ops:
  7.2 0.0 all-gather.3.cloned.1.call-start
  7.2 0.9 copy.41
  8.2 7.6 %all_to_all.15 = bf16[32,2,8,128]{3,0,1,2:T(8,128)(2,1)S(1)} all-to-all(bf16[32,2,8,128]{3,0,1,2:T(8,128)(2,1)S(1)} %copy.41), channel_id=1, replica_groups=mesh['ctx'=64,'tp'=4] {'tp'}, dimensions={2} | all-to-all | bytes 262144 | tf_op jit(solution)/shard_map/all_to_all | solution.py:16
  15.7 0.1 copy.56
  15.9 0.7 reshape.33
  16.6 0.0 all-gather.3.cloned.1.call-update
  16.6 158.0 %all-gather = s32[64,1,128]{2,1,0:T(1,128)S(1)} all-gather(s32[1,1,128]{2,1,0:T(1,128)} %bitcast.46), channel_id=1, replica_groups=mesh['ctx'=64,'tp'=4] {'ctx'}, dimensions={0}, use_global_device_ids=true | all-gather | bytes 33280 | tf_op jit(solution)/shard_map/all_gather | solution.py:19
  174.6 5.0 %fusion.10 = (pred[128,8192]{0,1:T(8,128)(4,1)S(1)}, pred[]{:T(512)}) fusion(s32[128]{0:T(128)} %param.7, s32[128]{0:T(128)S(1)} %iota_add_fusion, s32[8192]{0:T(1024)S(1)} %bitcast.45), kind=kLoop, calls=%fused_computation.15 | loop fusion | flops 4194303 | bytes 1082369 | tf_op jit(solution)/shard_map/and | solution.py:50
  180.3 151.4 %all-gather.3.cloned.1.call-done = bf16[8192,512]{1,0:T(8,128)(2,1)} async-done(((bf16[128,512]{1,0:T(8,128)(2,1)}), bf16[8192,512]{1,0:T(8,128)(2,1)}) %all-gather.3.cloned.1.call-update) | async-done | bytes 8388624 | tf_op jit(solution)/shard_map/all_gather | solution.py:46
  331.7 78.2 %conditional.1 = (f32[2,6,128]{2,1,0:T(8,128)}, f32[2,6,128]{2,1,0:T(8,128)}, f32[2,6,128]{2,1,0:T(8,128)S(1)}, f32[2,6,128,128]{2,3,1,0:T(8,128)S(1)}) conditional(s32[]{:T(128)} %convert_element_type.9, () %tuple.18, (pred[128,8192]{0,1:T(8,128)(4,1)S(1)}, bf16[8192,512]{1,0:T(8,128)(2,1)}, bf16[128,1536]{1,0:T(8,128)(2,1)}) %tuple.19), branch_computations={%region_1.0_spmd, %region_2.5_spmd} | conditional | flops 6606027264 | bytes 181323808 | solution.py:53
  331.7 1.2 copy.44
  332.9 12.0 %copy.43 = bf16[8192,512]{0,1:T(8,128)(2,1)} copy(bf16[8192,512]{1,0:T(8,128)(2,1)} %get-tuple-element.40) | data formatting | bytes 16777216 | tf_op jit(solution)/shard_map
  344.9 20.9 %fusion = (f32[2,6,128]{2,1,0:T(8,128)S(1)}, f32[2,8192,128,6]{2,1,3,0:T(8,128)}) fusion(pred[128,8192]{0,1:T(8,128)(4,1)S(1)} %get-tuple-element.9, bf16[128,2,6,128]{0,3,2,1:T(8,128)(2,1)S(1)} %bitcast.44, bf16[8192,2,2,128]{0,3,2,1:T(8,128)(2,1)} %bitcast.39), kind=kOutput, calls=%fused_computation.2 | convolution fusion | flops 3258972672 | bytes 55973888 | tf_op jit(solution)/shard_map/cond/branch_1_fun/qhgd,khd->hgqk/dot_general | solution.py:28
  365.8 0.6 broadcast_maximum_fusion
  366.4 20.4 %fusion.3 = f32[2,6,128,128]{2,3,1,0:T(8,128)S(1)} fusion(f32[2,8192,128,6]{2,1,3,0:T(8,128)} %get-tuple-element.46, f32[2,6,128]{2,1,0:T(8,128)} %broadcast_maximum_fusion, pred[128,8192]{0,1:T(8,128)(4,1)S(1)} %get-tuple-element.9, bf16[8192,2,2,128]{0,3,2,1:T(8,128)(2,1)} %bitcast.40), kind=kOutput, calls=%fused_computation.5 | convolution fusion | flops 3284140032 | bytes 56369152 | tf_op jit(solution)/shard_map/cond | solution.py:53
  386.9 22.3 %fusion.2 = f32[2,6,128]{2,1,0:T(8,128)} fusion(f32[2,8192,128,6]{2,1,3,0:T(8,128)} %get-tuple-element.46, f32[2,6,128]{2,1,0:T(8,128)} %broadcast_maximum_fusion, pred[128,8192]{0,1:T(8,128)(4,1)S(1)} %get-tuple-element.9), kind=kLoop, calls=%fused_computation.4 | loop fusion | flops 62913024 | bytes 51392512 | tf_op jit(solution)/shard_map/cond/branch_1_fun/reduce_sum | solution.py:36
  409.2 0.7 log.5
  409.9 0.8 divide_convert_fusion
  410.7 0.9 copy.46
  411.6 0.7 add.15
  412.3 0.6 reshape.35
  (1 shorter events, 0.0 us)
Async XLA Ops:
  7.2 324.5 %all-gather.3.cloned.1.call-start = ((), (), s32[]{:S(2)}) async-start(), calls=%async_computation.1 | async-start | bytes 8519680 | tf_op jit(solution)/shard_map/all_gather | solution.py:46
Sparse Core Ops, SparseCore 0:
  16.7 314.9 all-gather.2
where the time goes:
time: 421 us; the launch traced here: 420 us
  blocking collectives  166 us (39%)
  waiting for transfers between devices  151 us (36%)
  matrix products  41.3 us (10%)
  other arithmetic  29.4 us (7%)
  local copies, waits for them, and re-layouts  17.3 us (4%)
  between operations  14.7 us (3%)
    all_gather x1, blocking collectives, shards(): all_segments = lax.all_gather(segment_ids, 'ctx', axis=0, tiled=True)  158 us
    all_gather x1, waiting for transfers between devices, shards(): piece = lax.all_gather(own_block, 'ctx', axis=0, tiled=True)  151 us
    reduce_sum x1, other arithmetic, update(): total = jnp.sum(weights, axis=-1)  22.3 us
    dot_general x1, matrix products, update(): jnp.einsum('qhgd,khd->hgqk', query_heads, keys, preferred_element_type=jn...  20.9 us
    cond x1, matrix products, shards(): lax.cond(jnp.any(allowed), lambda inner: update(inner, pieces, allowed),...  20.4 us
    another operation x2, local copies, waits for them, and re-layouts  13.2 us
  transfers between devices with their start and end apart: 1, of which 1 were waited for; matrix products, arithmetic and copies ran while one was open for 1% of the time, Pallas kernels for 0%

commit v1 on v0

v1 whole, which is shorter than its diff:
```python
import jax
import jax.numpy as jnp
from jax import lax
from jax.experimental import pallas as pl
from jax.experimental.pallas import tpu as pltpu
from jax.sharding import PartitionSpec as P

Q_HEADS = 48
KV_HEADS = 8
HEAD = 128
GROUP = Q_HEADS // KV_HEADS
WIDE = GROUP * HEAD
Z, YL, X, YH, CORES = 8, 2, 4, 2, 2
PIECE = 64
ROWS = GROUP * PIECE
KS = 272
PART = 528
FACTOR = HEAD ** (-0.5)
SLOPE = FACTOR * 1.4426950408889634
LOW = -1e30
MESH = pl.DeviceIdType.MESH


def kernel(
    q_ref, kvp_ref, out_ref, lse_ref,
    qbuf, stage, kv, qseg, acc, top, total, outbuf, lsend, lrecv,
    s1_send, s1_recv, q_send, q_recv, o_send, o_recv, l_send, l_recv,
    za_send, za_recv, zb_send, zb_recv, y_send, y_recv,
    sa_send, sa_recv, sb_send, sb_recv, sc_send, sc_recv,
):
    ctx = lax.axis_index("ctx")
    tp = lax.axis_index("tp")
    z, yl, x = ctx // 8, (ctx // 4) % 2, ctx % 4
    yh, c = tp // 2, tp % 2

    def dev(z_, yl_, x_, yh_, c_):
        return (z_ * 8 + yl_ * 4 + x_, yh_ * 2 + c_)

    z_up, z_down = (z + 1) % 8, (z + 7) % 8
    up_dev = dev(z_up, yl, x, yh, c)
    down_dev = dev(z_down, yl, x, yh, c)
    y_dev = dev(z, 1 - yl, x, yh, c)
    core_dev = dev(z, yl, x, yh, 1 - c)

    barrier = pltpu.get_barrier_semaphore()
    for dx in range(4):
        for dt in range(4):
            if dx or dt:
                to = (z * 8 + yl * 4 + (x + dx) % 4, (tp + dt) % 4)
                pl.semaphore_signal(barrier, inc=1, device_id=to, device_id_type=MESH)
    for to in (up_dev, down_dev, y_dev):
        pl.semaphore_signal(barrier, inc=1, device_id=to, device_id_type=MESH)
    pl.semaphore_wait(barrier, 18)

    def remote(src, dst, ssem, rsem, to):
        return pltpu.make_async_remote_copy(
            src_ref=src, dst_ref=dst, send_sem=ssem, recv_sem=rsem, device_id=to, device_id_type=MESH
        )

    def s1_copy(i):
        x2, yh2 = (x + i % 4) % 4, (yh + i // 4) % 2
        return remote(
            kvp_ref.at[yh2 * 4 + x2], stage.at[x * 2 + c], s1_send.at[i], s1_recv.at[x * 2 + c],
            dev(z, yl, x2, yh2, yh),
        )

    def s1_local():
        return pltpu.make_async_copy(kvp_ref.at[yh * 4 + x], stage.at[x * 2 + c], s1_recv.at[x * 2 + c])

    def q_parts(i):
        r, c2 = i // 2, (c + i % 2) % 2
        src = q_ref.at[
            pl.ds(pl.multiple_of(c2 * PIECE, PIECE), PIECE), r * WIDE:(r + 1) * WIDE
        ]
        return src, 2 * c + r, c2

    def q_copy(i):
        src, x2, c2 = q_parts(i)
        return remote(src, qbuf.at[x], q_send.at[i], q_recv.at[x], dev(z, yl, x2, yh, c2))

    def q_local(i):
        return pltpu.make_async_copy(q_parts(i)[0], qbuf.at[x], q_recv.at[x])

    def q_mine(i):
        return (2 * c + i // 2 == x) if i % 2 == 0 else (c != c)

    s1_mine = c == yh
    pl.when(s1_mine)(lambda: s1_local().start())
    pl.when(jnp.logical_not(s1_mine))(lambda: s1_copy(0).start())
    for i in range(1, 8):
        s1_copy(i).start()
    for i in range(4):
        if i % 2:
            q_copy(i).start()
        else:
            pl.when(q_mine(i))(lambda i=i: q_local(i).start())
            pl.when(jnp.logical_not(q_mine(i)))(lambda i=i: q_copy(i).start())

    acc[...] = jnp.zeros_like(acc)
    total[...] = jnp.zeros_like(total)
    top[...] = jnp.full_like(top, LOW)

    lane16 = lax.broadcasted_iota(jnp.int32, (16, 128), 1)
    row16 = lax.broadcasted_iota(jnp.int32, (16, 128), 0)
    lane64 = lax.broadcasted_iota(jnp.int32, (PIECE, 128), 1)
    row64 = lax.broadcasted_iota(jnp.int32, (PIECE, 128), 0)

    for i in range(8):
        pltpu.make_async_copy(stage.at[i], stage.at[i], s1_recv.at[i]).wait()
    mine = kv.at[z, yl, c]
    segs = []
    for x2 in range(4):
        for c2 in range(2):
            at = x2 * 64 + c2 * 32
            mine[at:at + 32, :] = stage[x2 * 2 + c2, 0:32, :]
            mine[KS + at:KS + at + 32, :] = stage[x2 * 2 + c2, 32:64, :]
        seg = stage[x2 * 2, 64:80, :].astype(jnp.float32)
        turned = pltpu.roll(seg, 64, axis=1)
        stay = c == x2 % 2
        segs.append(jnp.where(stay, seg, turned))
        column = jnp.sum(
            jnp.where(lane64 == row64 + c * 64, jnp.concatenate([seg] * 4, 0), 0.0), axis=1, keepdims=True
        )
        qseg[x2] = jnp.broadcast_to(column, (PIECE, 128))
    first = jnp.where(lane16 < 64, segs[0], segs[1])
    second = jnp.where(lane16 < 64, segs[2], segs[3])
    mine[256:KS, :] = jnp.where(row16 == 0, first, second).astype(jnp.bfloat16)

    def level(d, k):
        return z - k if d == 0 else (z + k) % 8

    def arrives(d, k):
        if d == 0:
            return z - k >= 0
        return (level(1, k) <= 2) & (k <= 3) & (k >= 1)

    def used(d, k):
        if d == 0:
            return z - k >= 0
        return arrives(1, k) & (level(1, k) < z)

    def leaves(d, k):
        if d == 0:
            return (z - k >= 0) & (z < 7) & (k <= 3)
        return (level(1, k) <= 2) & (k <= 2)

    def za(d, k):
        ref = kv.at[level(d, k), yl, c]
        return remote(ref, ref, za_send.at[d, k], za_recv.at[d, k + 1], (up_dev, down_dev)[d])

    def zb(d, k):
        ref = kv.at[level(d, k), 1 - yl, c, KS:PART]
        return remote(ref, ref, zb_send.at[d, k], zb_recv.at[d, k + 1], (up_dev, down_dev)[d])

    def yc(d, k, whole=False):
        ref = kv.at[level(d, k), yl, c] if whole else kv.at[level(d, k), yl, c, 0:KS]
        return remote(ref, ref, y_send.at[d, k], y_recv.at[d, k], y_dev)

    def sa(d, k):
        ref = kv.at[level(d, k), yl, c]
        return remote(ref, ref, sa_send.at[d, k], sa_recv.at[d, k], core_dev)

    def sb(d, k, whole=False):
        ref = kv.at[level(d, k), 1 - yl, c]
        if not whole:
            ref = ref.at[KS:PART]
        return remote(ref, ref, sb_send.at[d, k], sb_recv.at[d, k], core_dev)

    def sc(d, k):
        ref = kv.at[level(d, k), 1 - yl, c, 0:KS]
        return remote(ref, ref, sc_send.at[d, k], sc_recv.at[d, k], core_dev)

    def got(ref, sem):
        pltpu.make_async_copy(ref, ref, sem).wait()

    def pump_z(k):
        for d in range(2):
            @pl.when(arrives(d, k))
            def _():
                got(kv.at[level(d, k), yl, c], za_recv.at[d, k])
                pl.when(leaves(d, k))(lambda: za(d, k).start())
            @pl.when(used(d, k))
            def _():
                yc(d, k).start()
                sa(d, k).start()
        for d in range(2):
            @pl.when(arrives(d, k))
            def _():
                got(kv.at[level(d, k), 1 - yl, c, KS:PART], zb_recv.at[d, k])
                pl.when(leaves(d, k))(lambda: zb(d, k).start())
            @pl.when(used(d, k))
            def _():
                sb(d, k).start()

    def pump_y(k):
        for d in range(2):
            @pl.when(used(d, k))
            def _():
                got(kv.at[level(d, k), 1 - yl, c, 0:KS], y_recv.at[d, k])
                sc(d, k).start()

    def pump_core(k):
        for d in range(2):
            @pl.when(used(d, k))
            def _():
                got(kv.at[level(d, k), yl, 1 - c], sa_recv.at[d, k])
                got(kv.at[level(d, k), 1 - yl, 1 - c, KS:PART], sb_recv.at[d, k])
                got(kv.at[level(d, k), 1 - yl, 1 - c, 0:KS], sc_recv.at[d, k])

    yc(0, 0, True).start()
    sa(0, 0).start()
    for d in range(2):
        pl.when(leaves(d, 0))(lambda d=d: za(d, 0).start())
    got(kv.at[z, 1 - yl, c], y_recv.at[0, 0])
    for d in range(2):
        pl.when(leaves(d, 0))(lambda d=d: zb(d, 0).start())
    sb(0, 0, True).start()

    for i in range(4):
        got(qbuf.at[i], q_recv.at[i])
    got(kv.at[z, yl, 1 - c], sa_recv.at[0, 0])
    got(kv.at[z, 1 - yl, 1 - c], sb_recv.at[0, 0])

    blocks = [(a, b) for a in range(2) for b in range(2)]

    def scores(tile, lv):
        q = jnp.concatenate([qbuf[tile, :, g * HEAD:(g + 1) * HEAD] for g in range(GROUP)], 0)
        keys = jnp.concatenate([kv[lv, a, b, 0:256, :] for a, b in blocks], 0)
        return lax.dot_general(q, keys, (((1,), (1,)), ((), ())), preferred_element_type=jnp.float32)

    def bias(tile, lv, causal):
        own = qseg[tile]
        parts = []
        for a, b in blocks:
            rows = kv[lv, a, b, 256:KS, :].astype(jnp.float32)
            for half in range(2):
                same = own == rows[half:half + 1, :]
                if causal:
                    place = a * 512 + (half * 2 + lane64 // 64) * 128 + b * 64 + lane64 % 64
                    same = same & (place <= yl * 512 + tile * 128 + c * 64 + row64)
                parts.append(jnp.where(same, 0.0, LOW))
        return jnp.concatenate(parts, 1)

    def absorb(tile, lv, s, causal):
        s = s + jnp.concatenate([bias(tile, lv, causal)] * GROUP, 0)
        before = top[tile]
        now = jnp.maximum(before, jnp.max(s, axis=1, keepdims=True))
        top[tile] = now
        shrink = jnp.exp2((before - now) * SLOPE)
        weights = jnp.exp2((s - now[:, :1]) * SLOPE)
        total[tile] = total[tile] * shrink + jnp.sum(weights, axis=1, keepdims=True)
        values = jnp.concatenate([kv[lv, a, b, KS:PART, :] for a, b in blocks], 0)
        acc[tile] = acc[tile] * shrink + jnp.dot(
            weights.astype(jnp.bfloat16), values, preferred_element_type=jnp.float32
        )

    def compute(lv, causal=False):
        s = scores(0, lv)
        for tile in range(4):
            later = scores(tile + 1, lv) if tile < 3 else None
            absorb(tile, lv, s, causal)
            s = later

    compute(z, True)

    def step(k, carry):
        @pl.when((k >= 2) & used(0, k - 1))
        def _():
            compute(level(0, k - 1))

        pl.when(k <= 4)(lambda: pump_z(k))

        @pl.when(used(1, k - 1))
        def _():
            compute(level(1, k - 1))

        @pl.when(k <= 4)
        def _():
            pump_y(k)
            pump_core(k)

        return carry

    lax.fori_loop(1, 6, step, 0)

    r, home = x % 2, x // 2

    def o_copy(tile):
        dst = out_ref.at[
            pl.ds(pl.multiple_of(c * PIECE, PIECE), PIECE), pl.ds(pl.multiple_of(r * WIDE, WIDE), WIDE)
        ]
        return outbuf.at[tile], dst, o_send.at[tile], o_recv.at[r * 2 + c], dev(z, yl, tile, yh, home)

    def l_copy(tile):
        return (
            lsend.at[tile], lrecv.at[r * 2 + c], l_send.at[tile], l_recv.at[r * 2 + c],
            dev(z, yl, tile, yh, home),
        )

    for tile in range(4):
        sums = total[tile]
        done = (acc[tile] * (1.0 / sums)).astype(jnp.bfloat16)
        logs = top[tile] * FACTOR + jnp.log(sums)
        lines = jnp.zeros((16, 128), jnp.float32)
        for g in range(GROUP):
            outbuf[tile, :, g * HEAD:(g + 1) * HEAD] = done[g * PIECE:(g + 1) * PIECE, :]
            line = jnp.sum(
                jnp.where(lane64 == row64 + c * 64, logs[g * PIECE:(g + 1) * PIECE, :], 0.0),
                axis=0, keepdims=True,
            )
            lines = lines + jnp.where(row16 == r * GROUP + g, line, 0.0)
        lsend[tile] = lines
        here = (tile == x) & (home == c)

        @pl.when(here)
        def _():
            for src, dst, _, rsem, _ in (o_copy(tile), l_copy(tile)):
                pltpu.make_async_copy(src, dst, rsem).start()

        @pl.when(jnp.logical_not(here))
        def _():
            for copy in (o_copy(tile), l_copy(tile)):
                remote(*copy).start()

    pl.when(jnp.logical_not(s1_mine))(lambda: s1_copy(0).wait_send())
    for i in range(1, 8):
        s1_copy(i).wait_send()
    for i in range(4):
        if i % 2:
            q_copy(i).wait_send()
        else:
            pl.when(jnp.logical_not(q_mine(i)))(lambda i=i: q_copy(i).wait_send())
    yc(0, 0, True).wait_send()
    sa(0, 0).wait_send()
    sb(0, 0, True).wait_send()
    for d in range(2):
        @pl.when(leaves(d, 0))
        def _():
            za(d, 0).wait_send()
            zb(d, 0).wait_send()

    def drain(k, carry):
        for d in range(2):
            @pl.when(arrives(d, k) & leaves(d, k))
            def _():
                za(d, k).wait_send()
                zb(d, k).wait_send()
            @pl.when(used(d, k))
            def _():
                yc(d, k).wait_send()
                sa(d, k).wait_send()
                sb(d, k).wait_send()
                sc(d, k).wait_send()
        return carry

    lax.fori_loop(1, 5, drain, 0)
    for tile in range(4):
        @pl.when(jnp.logical_not((tile == x) & (home == c)))
        def _():
            remote(*o_copy(tile)).wait_send()
            remote(*l_copy(tile)).wait_send()
    for i in range(4):
        got(lrecv.at[i], l_recv.at[i])
    lse_ref[...] = (lrecv[0] + lrecv[1] + lrecv[2] + lrecv[3])[:2 * GROUP, :]
    for i in range(4):
        got(outbuf.at[i], o_recv.at[i])


def shards(queries, keys_values, segment_ids):
    pieces = jnp.transpose(keys_values, (2, 1, 0, 3)).reshape(KV_HEADS, 64, HEAD)
    marks = jnp.broadcast_to(segment_ids.astype(jnp.bfloat16)[None, None, :], (KV_HEADS, 16, 128))
    kvp = jnp.concatenate([pieces, marks], axis=1)
    dma = pltpu.SemaphoreType.DMA
    bf, f32 = jnp.bfloat16, jnp.float32
    return pl.pallas_call(
        kernel,
        out_shape=(
            jax.ShapeDtypeStruct((128, 2 * WIDE), bf),
            jax.ShapeDtypeStruct((2 * GROUP, 128), f32),
        ),
        in_specs=[pl.BlockSpec(memory_space=pl.ANY)] * 2,
        out_specs=(pl.BlockSpec(memory_space=pl.ANY), pl.BlockSpec(memory_space=pltpu.VMEM)),
        scratch_shapes=[
            pltpu.VMEM((4, PIECE, WIDE), bf),
            pltpu.VMEM((8, 80, 128), bf),
            pltpu.VMEM((Z, YL, CORES, PART, HEAD), bf),
            pltpu.VMEM((4, PIECE, 128), f32),
            pltpu.VMEM((4, ROWS, HEAD), f32),
            pltpu.VMEM((4, ROWS, 128), f32),
            pltpu.VMEM((4, ROWS, 128), f32),
            pltpu.VMEM((4, PIECE, WIDE), bf),
            pltpu.VMEM((4, 16, 128), f32),
            pltpu.VMEM((4, 16, 128), f32),
            dma((8,)), dma((8,)), dma((4,)), dma((4,)), dma((4,)), dma((4,)), dma((4,)), dma((4,)),
        ] + [dma((2, 5))] * 12,
        compiler_params=pltpu.CompilerParams(
            collective_id=0, has_side_effects=True, vmem_limit_bytes=48 * 2**20
        ),
        cost_estimate=pl.CostEstimate(flops=6 * 10**9, bytes_accessed=10**6, transcendentals=12 * 10**6),
    )(queries, kvp)


def solution(mesh):
    placed = (P("ctx", "tp"), P(("ctx", "tp"), None, None, None), P("ctx"))
    return jax.shard_map(
        shards,
        mesh=mesh,
        in_specs=placed,
        out_specs=(P("ctx", "tp"), P("tp", "ctx")),
        check_vma=False,
    )
```

time: 421 us -> 69.1 us (0.16)
  the two profiles are of different devices: /device:TPU:16 before, /device:TPU:225 now
where the time goes in v1:
time: 69.1 us; the launch traced here: 69 us
  Pallas kernels  65.4 us (95%)
  local copies, waits for them, and re-layouts  2.94 us (4%)
    pallas_call x1, Pallas kernels, shards(): pl.pallas_call(kernel, out_shape=(jax.ShapeDtypeStruct((128, 2 * WIDE), b...  65.4 us
    unnamed x6, local copies, waits for them, and re-layouts  1.99 us

profile of v1, /device:TPU:225, one launch (start us, length us, event | category | flops | bytes accessed | tf_op | source)
XLA Modules:
  0.0 69.0 jit_solution(5779834113843240123)
XLA Ops:
  0.6 0.0 copy-start.1
  0.6 0.0 copy-start
  0.6 0.6 copy-done.1
  1.3 0.9 %copy.5 = bf16[8,2,32,128]{3,2,1,0:T(8,128)(2,1)S(1)} copy(bf16[8,2,32,128]{3,0,1,2:T(8,128)(2,1)} %bitcast.3) | data formatting | bytes 262144 | tf_op jit(solution)/shard_map/transpose | solution.py:370
  2.3 0.0 copy-done
  2.3 65.4 %shard_map.50 = (bf16[128,1536]{1,0:T(8,128)(2,1)S(1)}, f32[12,128]{1,0:T(8,128)S(1)}) custom-call(bf16[128,1536]{1,0:T(8,128)(2,1)S(1)} %copy-done, bf16[8,80,128]{2,1,0:T(8,128)(2,1)S(1)} %pad_maximum_fusion.kvp_ref), custom_call_target="tpu_custom_call" | custom-call | flops 6000000000 | bytes 1000000 | tf_op jit(solution)/shard_map/pallas_call | solution.py:375
  67.6 0.7 %copy.8 = bf16[128,1536]{1,0:T(8,128)(2,1)} copy(bf16[128,1536]{1,0:T(8,128)(2,1)S(1)} %get-tuple-element.4) | data formatting | bytes 786432
  68.4 0.6 copy.9
  (3 shorter events, 0.0 us)
Async XLA Ops:
  0.6 0.7 copy-start.1
  0.6 1.6 %copy-start = (bf16[128,1536]{1,0:T(8,128)(2,1)S(1)}, bf16[128,1536]{1,0:T(8,128)(2,1)}, u32[]{:S(2)}) copy-start(bf16[128,1536]{1,0:T(8,128)(2,1)} %q_ref.1) | copy-start | bytes 1179652

commit v2 on v1

--- a/solution.py
+++ b/solution.py
@@ -12,7 +12,9 @@
 WIDE = GROUP * HEAD
 Z, YL, X, YH, CORES = 8, 2, 4, 2, 2
 PIECE = 64
-ROWS = GROUP * PIECE
+HALF = 32
+ROWS = GROUP * HALF
+TILES = 8
 KS = 272
 PART = 528
 FACTOR = HEAD ** (-0.5)
@@ -104,6 +106,8 @@
     row16 = lax.broadcasted_iota(jnp.int32, (16, 128), 0)
     lane64 = lax.broadcasted_iota(jnp.int32, (PIECE, 128), 1)
     row64 = lax.broadcasted_iota(jnp.int32, (PIECE, 128), 0)
+    lane32 = lax.broadcasted_iota(jnp.int32, (HALF, 128), 1)
+    row32 = lax.broadcasted_iota(jnp.int32, (HALF, 128), 0)
 
     for i in range(8):
         pltpu.make_async_copy(stage.at[i], stage.at[i], s1_recv.at[i]).wait()
@@ -146,181 +150,257 @@
 
     def za(d, k):
         ref = kv.at[level(d, k), yl, c]
-        return remote(ref, ref, za_send.at[d, k], za_recv.at[d, k + 1], (up_dev, down_dev)[d])
+        return remote(ref, ref, za_send.at[d], za_recv.at[d, k], (up_dev, down_dev)[d])
 
     def zb(d, k):
         ref = kv.at[level(d, k), 1 - yl, c, KS:PART]
-        return remote(ref, ref, zb_send.at[d, k], zb_recv.at[d, k + 1], (up_dev, down_dev)[d])
+        return remote(ref, ref, zb_send.at[d], zb_recv.at[d, k], (up_dev, down_dev)[d])
 
     def yc(d, k, whole=False):
         ref = kv.at[level(d, k), yl, c] if whole else kv.at[level(d, k), yl, c, 0:KS]
-        return remote(ref, ref, y_send.at[d, k], y_recv.at[d, k], y_dev)
+        return remote(ref, ref, y_send.at[d], y_recv.at[d, k], y_dev)
 
     def sa(d, k):
         ref = kv.at[level(d, k), yl, c]
-        return remote(ref, ref, sa_send.at[d, k], sa_recv.at[d, k], core_dev)
+        return remote(ref, ref, sa_send.at[d], sa_recv.at[d, k], core_dev)
 
     def sb(d, k, whole=False):
         ref = kv.at[level(d, k), 1 - yl, c]
         if not whole:
             ref = ref.at[KS:PART]
-        return remote(ref, ref, sb_send.at[d, k], sb_recv.at[d, k], core_dev)
+        return remote(ref, ref, sb_send.at[d], sb_recv.at[d, k], core_dev)
 
     def sc(d, k):
         ref = kv.at[level(d, k), 1 - yl, c, 0:KS]
-        return remote(ref, ref, sc_send.at[d, k], sc_recv.at[d, k], core_dev)
+        return remote(ref, ref, sc_send.at[d], sc_recv.at[d, k], core_dev)
 
     def got(ref, sem):
         pltpu.make_async_copy(ref, ref, sem).wait()
 
-    def pump_z(k):
+    def pump_a(k):
         for d in range(2):
+            @pl.when(leaves(d, k - 1))
+            def _():
+                za(d, k - 1).wait_send()
+
             @pl.when(arrives(d, k))
             def _():
-                got(kv.at[level(d, k), yl, c], za_recv.at[d, k])
+                got(kv.at[level(d, k), yl, c], za_recv.at[d, k - 1])
                 pl.when(leaves(d, k))(lambda: za(d, k).start())
+
+            if isinstance(k, int):
+                if d == 0:
+                    yc(0, 0, True).wait_send()
+                    sa(0, 0).wait_send()
+            else:
+                @pl.when(used(d, k - 1))
+                def _():
+                    yc(d, k - 1).wait_send()
+                    sa(d, k - 1).wait_send()
+
             @pl.when(used(d, k))
             def _():
                 yc(d, k).start()
                 sa(d, k).start()
+
+    def pump_b(k):
         for d in range(2):
+            @pl.when(leaves(d, k - 1))
+            def _():
+                zb(d, k - 1).wait_send()
+
             @pl.when(arrives(d, k))
             def _():
-                got(kv.at[level(d, k), 1 - yl, c, KS:PART], zb_recv.at[d, k])
+                got(kv.at[level(d, k), 1 - yl, c, KS:PART], zb_recv.at[d, k - 1])
                 pl.when(leaves(d, k))(lambda: zb(d, k).start())
+
+            if d == 0:
+                @pl.when(k == 1)
+                def _():
+                    sb(0, 0, True).wait_send()
+
+            @pl.when(used(d, k - 1) & (k >= 2))
+            def _():
+                sb(d, k - 1).wait_send()
+
             @pl.when(used(d, k))
             def _():
                 sb(d, k).start()
 
     def pump_y(k):
         for d in range(2):
+            @pl.when(used(d, k - 1) & (k >= 2))
+            def _():
+                sc(d, k - 1).wait_send()
+
             @pl.when(used(d, k))
             def _():
                 got(kv.at[level(d, k), 1 - yl, c, 0:KS], y_recv.at[d, k])
                 sc(d, k).start()
 
-    def pump_core(k):
+    def await_a(k):
         for d in range(2):
             @pl.when(used(d, k))
             def _():
                 got(kv.at[level(d, k), yl, 1 - c], sa_recv.at[d, k])
+
+    def await_b(k):
+        for d in range(2):
+            @pl.when(used(d, k))
+            def _():
                 got(kv.at[level(d, k), 1 - yl, 1 - c, KS:PART], sb_recv.at[d, k])
                 got(kv.at[level(d, k), 1 - yl, 1 - c, 0:KS], sc_recv.at[d, k])
 
     yc(0, 0, True).start()
-    sa(0, 0).start()
     for d in range(2):
         pl.when(leaves(d, 0))(lambda d=d: za(d, 0).start())
+    sa(0, 0).start()
     got(kv.at[z, 1 - yl, c], y_recv.at[0, 0])
     for d in range(2):
         pl.when(leaves(d, 0))(lambda d=d: zb(d, 0).start())
     sb(0, 0, True).start()
-
+    pump_a(1)
     for i in range(4):
         got(qbuf.at[i], q_recv.at[i])
     got(kv.at[z, yl, 1 - c], sa_recv.at[0, 0])
     got(kv.at[z, 1 - yl, 1 - c], sb_recv.at[0, 0])
 
-    blocks = [(a, b) for a in range(2) for b in range(2)]
-
-    def scores(tile, lv):
-        q = jnp.concatenate([qbuf[tile, :, g * HEAD:(g + 1) * HEAD] for g in range(GROUP)], 0)
-        keys = jnp.concatenate([kv[lv, a, b, 0:256, :] for a, b in blocks], 0)
+    def lanes(unit):
+        return [(lv, y, b) for lv, y in unit for b in range(2)]
+
+    def scores(tile, unit):
+        xt, h = tile
+        q = jnp.concatenate(
+            [qbuf[xt, h * HALF:(h + 1) * HALF, g * HEAD:(g + 1) * HEAD] for g in range(GROUP)], 0
+        )
+        keys = jnp.concatenate([kv[lv, y, b, 0:256, :] for lv, y, b in lanes(unit)], 0)
         return lax.dot_general(q, keys, (((1,), (1,)), ((), ())), preferred_element_type=jnp.float32)
 
-    def bias(tile, lv, causal):
-        own = qseg[tile]
+    def bias(tile, unit, causal):
+        xt, h = tile
+        own = qseg[xt, h * HALF:(h + 1) * HALF, :]
         parts = []
-        for a, b in blocks:
-            rows = kv[lv, a, b, 256:KS, :].astype(jnp.float32)
+        for lv, y, b in lanes(unit):
+            rows = kv[lv, y, b, 256:KS, :].astype(jnp.float32)
             for half in range(2):
                 same = own == rows[half:half + 1, :]
                 if causal:
-                    place = a * 512 + (half * 2 + lane64 // 64) * 128 + b * 64 + lane64 % 64
-                    same = same & (place <= yl * 512 + tile * 128 + c * 64 + row64)
+                    place = y * 512 + (half * 2 + lane32 // 64) * 128 + b * 64 + lane32 % 64
+                    same = same & (place <= yl * 512 + xt * 128 + c * 64 + h * HALF + row32)
                 parts.append(jnp.where(same, 0.0, LOW))
         return jnp.concatenate(parts, 1)
 
-    def absorb(tile, lv, s, causal):
-        s = s + jnp.concatenate([bias(tile, lv, causal)] * GROUP, 0)
-        before = top[tile]
+    def absorb(tile, unit, s, causal):
+        at = tile[0] * 2 + tile[1]
+        s = s + jnp.concatenate([bias(tile, unit, causal)] * GROUP, 0)
+        before = top[at]
         now = jnp.maximum(before, jnp.max(s, axis=1, keepdims=True))
-        top[tile] = now
+        top[at] = now
         shrink = jnp.exp2((before - now) * SLOPE)
         weights = jnp.exp2((s - now[:, :1]) * SLOPE)
-        total[tile] = total[tile] * shrink + jnp.sum(weights, axis=1, keepdims=True)
-        values = jnp.concatenate([kv[lv, a, b, KS:PART, :] for a, b in blocks], 0)
-        acc[tile] = acc[tile] * shrink + jnp.dot(
-            weights.astype(jnp.bfloat16), values, preferred_element_type=jnp.float32
-        )
-
-    def compute(lv, causal=False):
-        s = scores(0, lv)
-        for tile in range(4):
-            later = scores(tile + 1, lv) if tile < 3 else None
-            absorb(tile, lv, s, causal)
+        values = jnp.concatenate([kv[lv, y, b, KS:PART, :] for lv, y, b in lanes(unit)], 0)
+        values = jnp.concatenate([values, jnp.ones_like(values)], 1)
+        sums = jnp.dot(weights.astype(jnp.bfloat16), values, preferred_element_type=jnp.float32)
+        acc[at] = acc[at] * shrink + sums[:, :HEAD]
+        total[at] = total[at] * shrink + sums[:, HEAD:]
+
+    TILED = [(xt, h) for xt in range(4) for h in range(2)]
+
+    def compute(unit, tiles=TILED, causal=False, after=None):
+        s = scores(tiles[0], unit)
+        for i, tile in enumerate(tiles):
+            later = scores(tiles[i + 1], unit) if i + 1 < len(tiles) else None
+            absorb(tile, unit, s, causal)
+            if after is not None and i % 2:
+                after(i // 2)
             s = later
 
-    compute(z, True)
+    def both(k):
+        return used(0, k) & used(1, k)
+
+    def unit_a(k):
+        return [(level(0, k), yl), (level(1, k), yl)]
+
+    def unit_b(k):
+        two = both(k)
+        return [
+            (level(0, k), jnp.where(two, 1 - yl, yl)),
+            (jnp.where(two, level(1, k), level(0, k)), 1 - yl),
+        ]
+
+    compute([(z, 0), (z, 1)], causal=True)
 
     def step(k, carry):
         @pl.when((k >= 2) & used(0, k - 1))
         def _():
-            compute(level(0, k - 1))
-
-        pl.when(k <= 4)(lambda: pump_z(k))
-
-        @pl.when(used(1, k - 1))
-        def _():
-            compute(level(1, k - 1))
-
-        @pl.when(k <= 4)
-        def _():
-            pump_y(k)
-            pump_core(k)
-
+            compute(unit_b(k - 1))
+
+        pump_b(k)
+        await_a(k)
+        pl.when(both(k))(lambda: compute(unit_a(k), TILED[:4]))
+        pump_y(k)
+        pl.when(both(k))(lambda: compute(unit_a(k), TILED[4:]))
+        pl.when(k <= 3)(lambda: pump_a(k + 1))
+        await_b(k)
         return carry
 
-    lax.fori_loop(1, 6, step, 0)
+    lax.fori_loop(1, 5, step, 0)
 
     r, home = x % 2, x // 2
 
-    def o_copy(tile):
+    def block(i):
+        return (x + 1 + i) % 4
+
+    def o_copy(i):
         dst = out_ref.at[
             pl.ds(pl.multiple_of(c * PIECE, PIECE), PIECE), pl.ds(pl.multiple_of(r * WIDE, WIDE), WIDE)
         ]
-        return outbuf.at[tile], dst, o_send.at[tile], o_recv.at[r * 2 + c], dev(z, yl, tile, yh, home)
-
-    def l_copy(tile):
-        return (
-            lsend.at[tile], lrecv.at[r * 2 + c], l_send.at[tile], l_recv.at[r * 2 + c],
-            dev(z, yl, tile, yh, home),
-        )
-
-    for tile in range(4):
-        sums = total[tile]
-        done = (acc[tile] * (1.0 / sums)).astype(jnp.bfloat16)
-        logs = top[tile] * FACTOR + jnp.log(sums)
+        xt = block(i)
+        return outbuf.at[xt], dst, o_send.at[i], o_recv.at[r * 2 + c], dev(z, yl, xt, yh, home)
+
+    def l_copy(i):
+        xt = block(i)
+        return lsend.at[xt], lrecv.at[r * 2 + c], l_send.at[i], l_recv.at[r * 2 + c], dev(z, yl, xt, yh, home)
+
+    def finish(i):
+        xt = block(i)
         lines = jnp.zeros((16, 128), jnp.float32)
-        for g in range(GROUP):
-            outbuf[tile, :, g * HEAD:(g + 1) * HEAD] = done[g * PIECE:(g + 1) * PIECE, :]
-            line = jnp.sum(
-                jnp.where(lane64 == row64 + c * 64, logs[g * PIECE:(g + 1) * PIECE, :], 0.0),
-                axis=0, keepdims=True,
-            )
-            lines = lines + jnp.where(row16 == r * GROUP + g, line, 0.0)
-        lsend[tile] = lines
-        here = (tile == x) & (home == c)
-
-        @pl.when(here)
-        def _():
-            for src, dst, _, rsem, _ in (o_copy(tile), l_copy(tile)):
-                pltpu.make_async_copy(src, dst, rsem).start()
-
-        @pl.when(jnp.logical_not(here))
-        def _():
-            for copy in (o_copy(tile), l_copy(tile)):
-                remote(*copy).start()
+        for h in range(2):
+            sums = total[xt * 2 + h]
+            done = (acc[xt * 2 + h] * (1.0 / sums)).astype(jnp.bfloat16)
+            logs = top[xt * 2 + h] * FACTOR + jnp.log(sums)
+            for g in range(GROUP):
+                rows = slice(g * HALF, (g + 1) * HALF)
+                outbuf[xt, h * HALF:(h + 1) * HALF, g * HEAD:(g + 1) * HEAD] = done[rows, :]
+                line = jnp.sum(
+                    jnp.where(lane32 == row32 + c * 64 + h * HALF, logs[rows, :], 0.0),
+                    axis=0, keepdims=True,
+                )
+                lines = lines + jnp.where(row16 == r * GROUP + g, line, 0.0)
+        lsend[xt] = lines
+        if i < 3:
+            remote(*o_copy(i)).start()
+            remote(*l_copy(i)).start()
+        else:
+            @pl.when(home == c)
+            def _():
+                for src, dst, _, rsem, _ in (o_copy(i), l_copy(i)):
+                    pltpu.make_async_copy(src, dst, rsem).start()
+
+            @pl.when(home != c)
+            def _():
+                remote(*o_copy(i)).start()
+                remote(*l_copy(i)).start()
+
+    @pl.when(used(0, 4))
+    def _():
+        tiles = [(block(i), h) for i in range(4) for h in range(2)]
+        compute([(level(0, 4), 0), (level(0, 4), 1)], tiles, after=finish)
+
+    @pl.when(jnp.logical_not(used(0, 4)))
+    def _():
+        for i in range(4):
+            finish(i)
 
     pl.when(jnp.logical_not(s1_mine))(lambda: s1_copy(0).wait_send())
     for i in range(1, 8):
@@ -330,35 +410,23 @@
             q_copy(i).wait_send()
         else:
             pl.when(jnp.logical_not(q_mine(i)))(lambda i=i: q_copy(i).wait_send())
-    yc(0, 0, True).wait_send()
-    sa(0, 0).wait_send()
-    sb(0, 0, True).wait_send()
-    for d in range(2):
-        @pl.when(leaves(d, 0))
-        def _():
-            za(d, 0).wait_send()
-            zb(d, 0).wait_send()
-
-    def drain(k, carry):
-        for d in range(2):
-            @pl.when(arrives(d, k) & leaves(d, k))
-            def _():
-                za(d, k).wait_send()
-                zb(d, k).wait_send()
-            @pl.when(used(d, k))
-            def _():
-                yc(d, k).wait_send()
-                sa(d, k).wait_send()
-                sb(d, k).wait_send()
-                sc(d, k).wait_send()
-        return carry
-
-    lax.fori_loop(1, 5, drain, 0)
-    for tile in range(4):
-        @pl.when(jnp.logical_not((tile == x) & (home == c)))
-        def _():
-            remote(*o_copy(tile)).wait_send()
-            remote(*l_copy(tile)).wait_send()
+
+    @pl.when(used(0, 4))
+    def _():
+        yc(0, 4).wait_send()
+        sa(0, 4).wait_send()
+        sb(0, 4).wait_send()
+        sc(0, 4).wait_send()
+
+    for i in range(3):
+        remote(*o_copy(i)).wait_send()
+        remote(*l_copy(i)).wait_send()
+
+    @pl.when(home != c)
+    def _():
+        remote(*o_copy(3)).wait_send()
+        remote(*l_copy(3)).wait_send()
+
     for i in range(4):
         got(lrecv.at[i], l_recv.at[i])
     lse_ref[...] = (lrecv[0] + lrecv[1] + lrecv[2] + lrecv[3])[:2 * GROUP, :]
@@ -385,14 +453,14 @@
             pltpu.VMEM((8, 80, 128), bf),
             pltpu.VMEM((Z, YL, CORES, PART, HEAD), bf),
             pltpu.VMEM((4, PIECE, 128), f32),
-            pltpu.VMEM((4, ROWS, HEAD), f32),
-            pltpu.VMEM((4, ROWS, 128), f32),
-            pltpu.VMEM((4, ROWS, 128), f32),
+            pltpu.VMEM((TILES, ROWS, HEAD), f32),
+            pltpu.VMEM((TILES, ROWS, 128), f32),
+            pltpu.VMEM((TILES, ROWS, 128), f32),
             pltpu.VMEM((4, PIECE, WIDE), bf),
             pltpu.VMEM((4, 16, 128), f32),
             pltpu.VMEM((4, 16, 128), f32),
             dma((8,)), dma((8,)), dma((4,)), dma((4,)), dma((4,)), dma((4,)), dma((4,)), dma((4,)),
-        ] + [dma((2, 5))] * 12,
+        ] + [dma((2,)), dma((2, 4))] * 2 + [dma((2,)), dma((2, 5))] * 4,
         compiler_params=pltpu.CompilerParams(
             collective_id=0, has_side_effects=True, vmem_limit_bytes=48 * 2**20
         ),

time: 69.1 us -> 53 us (0.77); the launches traced: 69 us -> 52 us
  Pallas kernels: 65.4 us -> 48.4 us
    pallas_call x1, Pallas kernels: 65.4 us -> 48.4 us  [shards(): pl.pallas_call(kernel, out_shape=(jax.ShapeDtypeStruct((128, 2 * WIDE), b...]
where the time goes in v2:
time: 53 us; the launch traced here: 52 us
  Pallas kernels  48.4 us (91%)
  local copies, waits for them, and re-layouts  2.94 us (6%)
  between operations  0.67 us (1%)
    pallas_call x1, Pallas kernels, shards(): pl.pallas_call(kernel, out_shape=(jax.ShapeDtypeStruct((128, 2 * WIDE), b...  48.4 us
    unnamed x6, local copies, waits for them, and re-layouts  1.99 us

profile of v2, /device:TPU:225, one launch (start us, length us, event | category | flops | bytes accessed | tf_op | source)
XLA Modules:
  0.0 52.0 jit_solution(3160529731289661590)
XLA Ops:
  0.6 0.0 copy-start.1
  0.6 0.0 copy-start
  0.6 0.6 %copy-done.1 = s32[128]{0:T(128)S(1)} copy-done((s32[128]{0:T(128)S(1)}, s32[128]{0:T(128)}, u32[]{:S(2)}) %copy-start.1) | copy-done | bytes 536
  1.3 0.9 %copy.5 = bf16[8,2,32,128]{3,2,1,0:T(8,128)(2,1)S(1)} copy(bf16[8,2,32,128]{3,0,1,2:T(8,128)(2,1)} %bitcast.3) | data formatting | bytes 262144 | tf_op jit(solution)/shard_map/transpose | solution.py:438
  2.3 0.0 copy-done
  2.3 48.4 %shard_map.50 = (bf16[128,1536]{1,0:T(8,128)(2,1)S(1)}, f32[12,128]{1,0:T(8,128)S(1)}) custom-call(bf16[128,1536]{1,0:T(8,128)(2,1)S(1)} %copy-done, bf16[8,80,128]{2,1,0:T(8,128)(2,1)S(1)} %pad_maximum_fusion.kvp_ref), custom_call_target="tpu_custom_call" | custom-call | flops 6000000000 | bytes 1000000 | tf_op jit(solution)/shard_map/pallas_call | solution.py:443
  50.7 0.7 %copy.8 = bf16[128,1536]{1,0:T(8,128)(2,1)} copy(bf16[128,1536]{1,0:T(8,128)(2,1)S(1)} %get-tuple-element.4) | data formatting | bytes 786432
  51.4 0.6 %copy.9 = f32[12,128]{1,0:T(8,128)} copy(f32[12,128]{1,0:T(8,128)S(1)} %get-tuple-element.5) | data formatting | bytes 12288
  (3 shorter events, 0.0 us)
Async XLA Ops:
  0.6 0.7 %copy-start.1 = (s32[128]{0:T(128)S(1)}, s32[128]{0:T(128)}, u32[]{:S(2)}) copy-start(s32[128]{0:T(128)} %param.5) | copy-start | bytes 1540
  0.6 1.6 %copy-start = (bf16[128,1536]{1,0:T(8,128)(2,1)S(1)}, bf16[128,1536]{1,0:T(8,128)(2,1)}, u32[]{:S(2)}) copy-start(bf16[128,1536]{1,0:T(8,128)(2,1)} %q_ref.1) | copy-start | bytes 1179652

commit v3 on v2

v3 whole, which is shorter than its diff:
```python
import jax
import jax.numpy as jnp
from jax import lax
from jax.experimental import pallas as pl
from jax.experimental.pallas import tpu as pltpu
from jax.sharding import PartitionSpec as P

Q_HEADS = 48
KV_HEADS = 8
HEAD = 128
GROUP = Q_HEADS // KV_HEADS
WIDE = GROUP * HEAD
Z, YL, X, YH, CORES = 8, 2, 4, 2, 2
PIECE = 64
HALF = 32
ROWS = GROUP * HALF
TILES = 8
KS = 272
PART = 528
CUT = 352
FACTOR = HEAD ** (-0.5)
SLOPE = FACTOR * 1.4426950408889634
LOW = -1e30
MESH = pl.DeviceIdType.MESH


def kernel(
    q_ref, pieces, out_ref, lse_ref,
    qbuf, stage, kv, qseg, acc, top, total, outbuf, lsend, lrecv,
    s1_send, s1_recv, q_send, q_recv, o_send, o_recv, l_send, l_recv,
    za_send, za_recv, zb_send, zb_recv, y_send, y_recv, yb_send, yb_recv,
    sa_send, sa_recv, sb_send, sb_recv, sc_send, sc_recv,
):
    ctx = lax.axis_index("ctx")
    tp = lax.axis_index("tp")
    z, yl, x = ctx // 8, (ctx // 4) % 2, ctx % 4
    yh, c = tp // 2, tp % 2

    def dev(z_, yl_, x_, yh_, c_):
        return (z_ * 8 + yl_ * 4 + x_, yh_ * 2 + c_)

    z_up, z_down = (z + 1) % 8, (z + 7) % 8
    up_dev = dev(z_up, yl, x, yh, c)
    down_dev = dev(z_down, yl, x, yh, c)
    y_dev = dev(z, 1 - yl, x, yh, c)
    core_dev = dev(z, yl, x, yh, 1 - c)

    barrier = pltpu.get_barrier_semaphore()
    for dx in range(4):
        for dt in range(4):
            if dx or dt:
                to = (z * 8 + yl * 4 + (x + dx) % 4, (tp + dt) % 4)
                pl.semaphore_signal(barrier, inc=1, device_id=to, device_id_type=MESH)
    for to in (up_dev, down_dev, y_dev):
        pl.semaphore_signal(barrier, inc=1, device_id=to, device_id_type=MESH)

    acc[...] = jnp.zeros_like(acc)
    total[...] = jnp.zeros_like(total)
    top[...] = jnp.full_like(top, LOW)
    pl.semaphore_wait(barrier, 18)

    def remote(src, dst, ssem, rsem, to):
        return pltpu.make_async_remote_copy(
            src_ref=src, dst_ref=dst, send_sem=ssem, recv_sem=rsem, device_id=to, device_id_type=MESH
        )

    def s1_copy(i):
        x2, yh2 = (x + i % 4) % 4, (yh + i // 4) % 2
        return remote(
            pieces.at[yh2 * 4 + x2], stage.at[x * 2 + c], s1_send, s1_recv,
            dev(z, yl, x2, yh2, yh),
        )

    def s1_local():
        return pltpu.make_async_copy(pieces.at[yh * 4 + x], stage.at[x * 2 + c], s1_recv)

    def q_parts(i):
        r, c2 = i // 2, (c + i % 2) % 2
        src = q_ref.at[
            pl.ds(pl.multiple_of(c2 * PIECE, PIECE), PIECE), r * WIDE:(r + 1) * WIDE
        ]
        return src, 2 * c + r, c2

    def q_copy(i):
        src, x2, c2 = q_parts(i)
        return remote(src, qbuf.at[x], q_send, q_recv, dev(z, yl, x2, yh, c2))

    def q_local(i):
        return pltpu.make_async_copy(q_parts(i)[0], qbuf.at[x], q_recv)

    def q_mine(i):
        return (2 * c + i // 2 == x) if i % 2 == 0 else (c != c)

    s1_mine = c == yh
    pl.when(s1_mine)(lambda: s1_local().start())
    pl.when(jnp.logical_not(s1_mine))(lambda: s1_copy(0).start())
    for i in range(1, 8):
        s1_copy(i).start()
    lane16 = lax.broadcasted_iota(jnp.int32, (16, 128), 1)
    row16 = lax.broadcasted_iota(jnp.int32, (16, 128), 0)
    lane64 = lax.broadcasted_iota(jnp.int32, (PIECE, 128), 1)
    row64 = lax.broadcasted_iota(jnp.int32, (PIECE, 128), 0)
    lane32 = lax.broadcasted_iota(jnp.int32, (HALF, 128), 1)
    row32 = lax.broadcasted_iota(jnp.int32, (HALF, 128), 0)

    pltpu.make_async_copy(stage, stage, s1_recv).wait()
    mine = kv.at[z, yl, c]
    segs = []
    for x2 in range(4):
        for c2 in range(2):
            at = x2 * 64 + c2 * 32
            mine[at:at + 32, :] = stage[x2 * 2 + c2, 0:32, :]
            mine[KS + at:KS + at + 32, :] = stage[x2 * 2 + c2, 32:64, :]
        seg = stage[x2 * 2, 64:80, :].astype(jnp.float32)
        segs.append(jnp.where(c == x2 % 2, seg, pltpu.roll(seg, 64, axis=1)))
    first = jnp.where(lane16 < 64, segs[0], segs[1])
    second = jnp.where(lane16 < 64, segs[2], segs[3])
    mine[256:KS, :] = jnp.where(row16 == 0, first, second).astype(jnp.bfloat16)

    def level(d, k):
        return z - k if d == 0 else (z + k) % 8

    def arrives(d, k):
        if d == 0:
            return z - k >= 0
        return (level(1, k) <= 2) & (k <= 3) & (k >= 1)

    def used(d, k):
        if d == 0:
            return z - k >= 0
        return arrives(1, k) & (level(1, k) < z)

    def leaves(d, k):
        if d == 0:
            return (z - k >= 0) & (z < 7) & (k <= 3)
        return (level(1, k) <= 2) & (k <= 2)

    def za(d, k):
        ref = kv.at[level(d, k), yl, c, 0:CUT]
        return remote(ref, ref, za_send.at[d], za_recv.at[d, k], (up_dev, down_dev)[d])

    def zb(d, k, y):
        ref = kv.at[level(d, k), y, c, CUT:PART]
        return remote(ref, ref, zb_send.at[d], zb_recv.at[d, k], (up_dev, down_dev)[d])

    def yc(d, k):
        ref = kv.at[level(d, k), yl, c, 0:CUT]
        return remote(ref, ref, y_send.at[d], y_recv.at[d, k], y_dev)

    def y_rest():
        ref = kv.at[z, yl, c, CUT:PART]
        return remote(ref, ref, yb_send, yb_recv, y_dev)

    def sa(d, k):
        ref = kv.at[level(d, k), yl, c, 0:CUT]
        return remote(ref, ref, sa_send.at[d], sa_recv.at[d, k], core_dev)

    def sb(d, k, y):
        ref = kv.at[level(d, k), y, c, CUT:PART]
        return remote(ref, ref, sb_send.at[d], sb_recv.at[d, k], core_dev)

    def sc(d, k):
        ref = kv.at[level(d, k), 1 - yl, c, 0:CUT]
        return remote(ref, ref, sc_send.at[d], sc_recv.at[d, k], core_dev)

    def got(ref, sem):
        pltpu.make_async_copy(ref, ref, sem).wait()

    def got_two(sem):
        got(kv.at[0, 0, 0, 0:2 * (PART - CUT)], sem)

    def pump_a(k):
        for d in range(2):
            @pl.when(leaves(d, k - 1))
            def _():
                za(d, k - 1).wait_send()

            @pl.when(arrives(d, k))
            def _():
                got(kv.at[level(d, k), yl, c, 0:CUT], za_recv.at[d, k - 1])
                pl.when(leaves(d, k))(lambda: za(d, k).start())

            @pl.when(used(d, k - 1))
            def _():
                yc(d, k - 1).wait_send()
                sa(d, k - 1).wait_send()

            @pl.when(used(d, k))
            def _():
                yc(d, k).start()
                sa(d, k).start()

    def pump_b(k):
        for d in range(2):
            @pl.when(leaves(d, k - 1))
            def _():
                got_two(zb_send.at[d])

            @pl.when(arrives(d, k))
            def _():
                got_two(zb_recv.at[d, k - 1])

                @pl.when(leaves(d, k))
                def _():
                    zb(d, k, yl).start()
                    zb(d, k, 1 - yl).start()

            pl.when(used(d, k - 1))(lambda: got_two(sb_send.at[d]))

            @pl.when(used(d, k))
            def _():
                sb(d, k, yl).start()
                sb(d, k, 1 - yl).start()

    def pump_y(k):
        for d in range(2):
            pl.when(used(d, k - 1) & (k >= 1))(lambda: sc(d, k - 1).wait_send())

            @pl.when(used(d, k))
            def _():
                got(kv.at[level(d, k), 1 - yl, c, 0:CUT], y_recv.at[d, k])
                sc(d, k).start()

    def await_a(k):
        for d in range(2):
            @pl.when(used(d, k))
            def _():
                got(kv.at[level(d, k), yl, 1 - c, 0:CUT], sa_recv.at[d, k])
                got_two(sb_recv.at[d, k])

    def await_b(k):
        for d in range(2):
            @pl.when(used(d, k))
            def _():
                got(kv.at[level(d, k), 1 - yl, 1 - c, 0:CUT], sc_recv.at[d, k])

    for d in range(2):
        pl.when(leaves(d, 0))(lambda d=d: za(d, 0).start())
    y_rest().start()
    for d in range(2):
        pl.when(leaves(d, 0))(lambda d=d: zb(d, 0, yl).start())
    yc(0, 0).start()
    sa(0, 0).start()
    sb(0, 0, yl).start()
    for i in range(4):
        if i % 2:
            q_copy(i).start()
        else:
            pl.when(q_mine(i))(lambda i=i: q_local(i).start())
            pl.when(jnp.logical_not(q_mine(i)))(lambda i=i: q_copy(i).start())

    for x2 in range(4):
        seg = stage[x2 * 2, 64:80, :].astype(jnp.float32)
        column = jnp.sum(
            jnp.where(lane64 == row64 + c * 64, jnp.concatenate([seg] * 4, 0), 0.0), axis=1, keepdims=True
        )
        qseg[x2] = jnp.broadcast_to(column, (PIECE, 128))
    got(kv.at[z, 1 - yl, c, CUT:PART], yb_recv)
    for d in range(2):
        pl.when(leaves(d, 0))(lambda d=d: zb(d, 0, 1 - yl).start())
    sb(0, 0, 1 - yl).start()
    pump_y(0)

    def lanes(unit):
        return [(lv, y, b) for lv, y in unit for b in range(2)]

    def scores(tile, unit):
        xt, h = tile
        q = jnp.concatenate(
            [qbuf[xt, h * HALF:(h + 1) * HALF, g * HEAD:(g + 1) * HEAD] for g in range(GROUP)], 0
        )
        keys = jnp.concatenate([kv[lv, y, b, 0:256, :] for lv, y, b in lanes(unit)], 0)
        return lax.dot_general(q, keys, (((1,), (1,)), ((), ())), preferred_element_type=jnp.float32)

    def bias(tile, unit, causal):
        xt, h = tile
        own = qseg[xt, h * HALF:(h + 1) * HALF, :]
        parts = []
        for lv, y, b in lanes(unit):
            rows = kv[lv, y, b, 256:KS, :].astype(jnp.float32)
            for half in range(2):
                same = own == rows[half:half + 1, :]
                if causal:
                    place = y * 512 + (half * 2 + lane32 // 64) * 128 + b * 64 + lane32 % 64
                    same = same & (place <= yl * 512 + xt * 128 + c * 64 + h * HALF + row32)
                parts.append(jnp.where(same, 0.0, LOW))
        return jnp.concatenate(parts, 1)

    def absorb(tile, unit, s, causal):
        at = tile[0] * 2 + tile[1]
        s = s + jnp.concatenate([bias(tile, unit, causal)] * GROUP, 0)
        before = top[at]
        now = jnp.maximum(before, jnp.max(s, axis=1, keepdims=True))
        top[at] = now
        shrink = jnp.exp2((before - now) * SLOPE)
        weights = jnp.exp2((s - now[:, :1]) * SLOPE)
        values = jnp.concatenate([kv[lv, y, b, KS:PART, :] for lv, y, b in lanes(unit)], 0)
        values = jnp.concatenate([values, jnp.ones_like(values)], 1)
        sums = jnp.dot(weights.astype(jnp.bfloat16), values, preferred_element_type=jnp.float32)
        acc[at] = acc[at] * shrink + sums[:, :HEAD]
        total[at] = total[at] * shrink + sums[:, HEAD:]

    TILED = [(xt, h) for xt in range(4) for h in range(2)]

    def compute_all(items, causal=False):
        s = scores(*items[0][:2])
        for i, (tile, unit, after) in enumerate(items):
            later = scores(*items[i + 1][:2]) if i + 1 < len(items) else None
            absorb(tile, unit, s, causal)
            if after is not None:
                after()
            s = later

    def compute(unit, tiles=TILED, causal=False):
        compute_all([(tile, unit, None) for tile in tiles], causal)

    def both(k):
        return used(0, k) & used(1, k)

    def unit_a(k):
        return [(level(0, k), yl), (level(1, k), yl)]

    def unit_b(k):
        two = both(k)
        return [
            (level(0, k), jnp.where(two, 1 - yl, yl)),
            (jnp.where(two, level(1, k), level(0, k)), 1 - yl),
        ]

    pump_a(1)
    await_a(0)
    await_b(0)
    got(qbuf, q_recv)
    compute([(z, 0), (z, 1)], causal=True)
    pump_b(1)

    def step(k, carry):
        pump_a(k)
        await_a(k - 1)
        pl.when(both(k - 1))(lambda: compute(unit_a(k - 1)))
        pump_b(k)
        pump_y(k - 1)

        @pl.when(k >= 3)
        def _():
            await_b(k - 2)
            pl.when(used(0, k - 2))(lambda: compute(unit_b(k - 2)))
        return carry

    lax.fori_loop(2, 5, step, 0)

    r, home = x % 2, x // 2

    def block(i):
        return (x + (2, 1, 3, 0)[i]) % 4

    def o_copy(i, h):
        dst = out_ref.at[
            pl.ds(pl.multiple_of(c * PIECE + h * HALF, HALF), HALF),
            pl.ds(pl.multiple_of(r * WIDE, WIDE), WIDE),
        ]
        xt = block(i)
        return (
            outbuf.at[xt, h * HALF:(h + 1) * HALF], dst, o_send, o_recv,
            dev(z, yl, xt, yh, home),
        )

    def l_copy(i):
        xt = block(i)
        return lsend.at[xt], lrecv.at[r * 2 + c], l_send, l_recv, dev(z, yl, xt, yh, home)

    def leave(i, copy):
        if i < 3:
            remote(*copy).start()
        else:
            src, dst, _, rsem, _ = copy
            pl.when(home == c)(lambda: pltpu.make_async_copy(src, dst, rsem).start())
            pl.when(home != c)(lambda: remote(*copy).start())

    def finish(i, h):
        xt = block(i)
        lines = jnp.zeros((16, 128), jnp.float32) if h == 0 else lsend[xt]
        sums = total[xt * 2 + h]
        done = (acc[xt * 2 + h] * (1.0 / sums)).astype(jnp.bfloat16)
        logs = top[xt * 2 + h] * FACTOR + jnp.log(sums)
        for g in range(GROUP):
            rows = slice(g * HALF, (g + 1) * HALF)
            outbuf[xt, h * HALF:(h + 1) * HALF, g * HEAD:(g + 1) * HEAD] = done[rows, :]
            line = jnp.sum(
                jnp.where(lane32 == row32 + c * 64 + h * HALF, logs[rows, :], 0.0), axis=0, keepdims=True
            )
            lines = lines + jnp.where(row16 == r * GROUP + g, line, 0.0)
        lsend[xt] = lines
        leave(i, o_copy(i, h))
        if h == 1:
            leave(i, l_copy(i))

    pump_y(4)
    await_b(3)
    pl.when(used(0, 3))(lambda: compute(unit_b(3)))

    @pl.when(used(0, 4))
    def _():
        await_a(4)
        await_b(4)
        unit = [(level(0, 4), 0), (level(0, 4), 1)]
        compute_all([
            ((block(i), h), unit, lambda i=i, h=h: finish(i, h)) for i in range(4) for h in range(2)
        ])

    @pl.when(jnp.logical_not(used(0, 4)))
    def _():
        for i in range(4):
            for h in range(2):
                finish(i, h)

    pl.when(s1_mine)(lambda: got(stage.at[0:7], s1_send))
    pl.when(jnp.logical_not(s1_mine))(lambda: got(stage, s1_send))
    pl.when(home == c)(lambda: got(qbuf.at[0:3], q_send))
    pl.when(home != c)(lambda: got(qbuf, q_send))

    @pl.when(used(0, 4))
    def _():
        yc(0, 4).wait_send()
        sa(0, 4).wait_send()
        got_two(sb_send.at[0])
        sc(0, 4).wait_send()

    y_rest().wait_send()

    @pl.when(home == c)
    def _():
        got(outbuf.at[0:3], o_send)
        got(lsend.at[0:3], l_send)

    @pl.when(home != c)
    def _():
        got(outbuf, o_send)
        got(lsend, l_send)

    got(lrecv, l_recv)
    lse_ref[...] = (lrecv[0] + lrecv[1] + lrecv[2] + lrecv[3])[:2 * GROUP, :]
    got(outbuf, o_recv)


def shards(queries, keys_values, segment_ids):
    pieces = jnp.transpose(keys_values, (2, 1, 0, 3)).reshape(KV_HEADS, 64, HEAD)
    marks = jnp.broadcast_to(segment_ids.astype(jnp.bfloat16)[None, None, :], (KV_HEADS, 16, 128))
    kvp = jnp.concatenate([pieces, marks], axis=1)
    dma = pltpu.SemaphoreType.DMA
    bf, f32 = jnp.bfloat16, jnp.float32
    return pl.pallas_call(
        kernel,
        out_shape=(
            jax.ShapeDtypeStruct((128, 2 * WIDE), bf),
            jax.ShapeDtypeStruct((2 * GROUP, 128), f32),
        ),
        in_specs=[pl.BlockSpec(memory_space=pl.ANY)] * 2,
        out_specs=(pl.BlockSpec(memory_space=pl.ANY), pl.BlockSpec(memory_space=pltpu.VMEM)),
        scratch_shapes=[
            pltpu.VMEM((4, PIECE, WIDE), bf),
            pltpu.VMEM((8, 80, 128), bf),
            pltpu.VMEM((Z, YL, CORES, PART, HEAD), bf),
            pltpu.VMEM((4, PIECE, 128), f32),
            pltpu.VMEM((TILES, ROWS, HEAD), f32),
            pltpu.VMEM((TILES, ROWS, 128), f32),
            pltpu.VMEM((TILES, ROWS, 128), f32),
            pltpu.VMEM((4, PIECE, WIDE), bf),
            pltpu.VMEM((4, 16, 128), f32),
            pltpu.VMEM((4, 16, 128), f32),
            dma, dma, dma, dma, dma, dma, dma, dma,
        ] + [dma((2,)), dma((2, 4))] * 2 + [dma((2,)), dma((2, 5)), dma, dma] + [dma((2,)), dma((2, 5))] * 3,
        compiler_params=pltpu.CompilerParams(
            collective_id=0, has_side_effects=True, vmem_limit_bytes=48 * 2**20
        ),
        cost_estimate=pl.CostEstimate(flops=6 * 10**9, bytes_accessed=10**6, transcendentals=12 * 10**6),
    )(queries, kvp)


def solution(mesh):
    placed = (P("ctx", "tp"), P(("ctx", "tp"), None, None, None), P("ctx"))
    return jax.shard_map(
        shards,
        mesh=mesh,
        in_specs=placed,
        out_specs=(P("ctx", "tp"), P("tp", "ctx")),
        check_vma=False,
    )
```

time: 53 us -> 50.7 us (0.957); the launches traced: 52 us -> 50.6 us
  Pallas kernels: 48.4 us -> 46.9 us
    pallas_call x1, Pallas kernels: 48.4 us -> 46.9 us  [shards(): pl.pallas_call(kernel, out_shape=(jax.ShapeDtypeStruct((128, 2 * WIDE), b...]
where the time goes in v3:
time: 50.7 us; the launch traced here: 50.6 us
  Pallas kernels  46.9 us (93%)
  local copies, waits for them, and re-layouts  2.94 us (6%)
  between operations  0.67 us (1%)
    pallas_call x1, Pallas kernels, shards(): pl.pallas_call(kernel, out_shape=(jax.ShapeDtypeStruct((128, 2 * WIDE), b...  46.9 us
    unnamed x6, local copies, waits for them, and re-layouts  1.99 us

profile of v3, /device:TPU:225, one launch (start us, length us, event | category | flops | bytes accessed | tf_op | source)
XLA Modules:
  0.0 50.6 jit_solution(9554922407195506131)
XLA Ops:
  0.6 0.0 copy-start.1
  0.6 0.0 copy-start
  0.6 0.6 %copy-done.1 = s32[128]{0:T(128)S(1)} copy-done((s32[128]{0:T(128)S(1)}, s32[128]{0:T(128)}, u32[]{:S(2)}) %copy-start.1) | copy-done | bytes 536
  1.3 0.9 %copy.5 = bf16[8,2,32,128]{3,2,1,0:T(8,128)(2,1)S(1)} copy(bf16[8,2,32,128]{3,0,1,2:T(8,128)(2,1)} %bitcast.3) | data formatting | bytes 262144 | tf_op jit(solution)/shard_map/transpose | solution.py:447
  2.3 0.0 copy-done
  2.3 46.9 %shard_map.50 = (bf16[128,1536]{1,0:T(8,128)(2,1)S(1)}, f32[12,128]{1,0:T(8,128)S(1)}) custom-call(bf16[128,1536]{1,0:T(8,128)(2,1)S(1)} %copy-done, bf16[8,80,128]{2,1,0:T(8,128)(2,1)S(1)} %pad_maximum_fusion.pieces), custom_call_target="tpu_custom_call" | custom-call | flops 6000000000 | bytes 1000000 | tf_op jit(solution)/shard_map/pallas_call | solution.py:452
  49.2 0.7 %copy.8 = bf16[128,1536]{1,0:T(8,128)(2,1)} copy(bf16[128,1536]{1,0:T(8,128)(2,1)S(1)} %get-tuple-element.4) | data formatting | bytes 786432
  50.0 0.6 %copy.9 = f32[12,128]{1,0:T(8,128)} copy(f32[12,128]{1,0:T(8,128)S(1)} %get-tuple-element.5) | data formatting | bytes 12288
  (3 shorter events, 0.0 us)
Async XLA Ops:
  0.6 0.7 %copy-start.1 = (s32[128]{0:T(128)S(1)}, s32[128]{0:T(128)}, u32[]{:S(2)}) copy-start(s32[128]{0:T(128)} %param.5) | copy-start | bytes 1540
  0.6 1.6 %copy-start = (bf16[128,1536]{1,0:T(8,128)(2,1)S(1)}, bf16[128,1536]{1,0:T(8,128)(2,1)}, u32[]{:S(2)}) copy-start(bf16[128,1536]{1,0:T(8,128)(2,1)} %q_ref.1) | copy-start | bytes 1179652

commit v4 on v3

--- a/solution.py
+++ b/solution.py
@@ -331,20 +331,23 @@
     await_a(0)
     await_b(0)
     got(qbuf, q_recv)
+    pump_b(1)
     compute([(z, 0), (z, 1)], causal=True)
-    pump_b(1)
 
     def step(k, carry):
         pump_a(k)
+        pump_y(k - 1)
         await_a(k - 1)
         pl.when(both(k - 1))(lambda: compute(unit_a(k - 1)))
         pump_b(k)
-        pump_y(k - 1)
-
-        @pl.when(k >= 3)
+        pl.when(k == 4)(lambda: pump_y(4))
+        done = k - 1
+
+        @pl.when((done >= 1) & used(0, done))
         def _():
-            await_b(k - 2)
-            pl.when(used(0, k - 2))(lambda: compute(unit_b(k - 2)))
+            await_b(done)
+            compute(unit_b(done))
+
         return carry
 
     lax.fori_loop(2, 5, step, 0)
@@ -395,9 +398,6 @@
         if h == 1:
             leave(i, l_copy(i))
 
-    pump_y(4)
-    await_b(3)
-    pl.when(used(0, 3))(lambda: compute(unit_b(3)))
 
     @pl.when(used(0, 4))
     def _():

time: 50.7 us -> 49.3 us (0.972)
  Pallas kernels: 46.9 us -> 45.5 us
    pallas_call x1, Pallas kernels: 46.9 us -> 45.5 us  [shards(): pl.pallas_call(kernel, out_shape=(jax.ShapeDtypeStruct((128, 2 * WIDE), b...]
where the time goes in v4:
time: 49.3 us; the launch traced here: 49.2 us
  Pallas kernels  45.5 us (92%)
  local copies, waits for them, and re-layouts  2.94 us (6%)
  between operations  0.67 us (1%)
    pallas_call x1, Pallas kernels, shards(): pl.pallas_call(kernel, out_shape=(jax.ShapeDtypeStruct((128, 2 * WIDE), b...  45.5 us
    unnamed x6, local copies, waits for them, and re-layouts  1.99 us

profile of v4, /device:TPU:225, one launch (start us, length us, event | category | flops | bytes accessed | tf_op | source)
XLA Modules:
  0.0 49.2 jit_solution(4854735686908528862)
XLA Ops:
  0.6 0.0 copy-start.1
  0.6 0.0 copy-start
  0.6 0.6 %copy-done.1 = s32[128]{0:T(128)S(1)} copy-done((s32[128]{0:T(128)S(1)}, s32[128]{0:T(128)}, u32[]{:S(2)}) %copy-start.1) | copy-done | bytes 536
  1.3 0.9 %copy.5 = bf16[8,2,32,128]{3,2,1,0:T(8,128)(2,1)S(1)} copy(bf16[8,2,32,128]{3,0,1,2:T(8,128)(2,1)} %bitcast.3) | data formatting | bytes 262144 | tf_op jit(solution)/shard_map/transpose | solution.py:447
  2.3 0.0 copy-done
  2.3 45.5 %shard_map.50 = (bf16[128,1536]{1,0:T(8,128)(2,1)S(1)}, f32[12,128]{1,0:T(8,128)S(1)}) custom-call(bf16[128,1536]{1,0:T(8,128)(2,1)S(1)} %copy-done, bf16[8,80,128]{2,1,0:T(8,128)(2,1)S(1)} %pad_maximum_fusion.pieces), custom_call_target="tpu_custom_call" | custom-call | flops 6000000000 | bytes 1000000 | tf_op jit(solution)/shard_map/pallas_call | solution.py:452
  47.8 0.7 %copy.8 = bf16[128,1536]{1,0:T(8,128)(2,1)} copy(bf16[128,1536]{1,0:T(8,128)(2,1)S(1)} %get-tuple-element.4) | data formatting | bytes 786432
  48.6 0.6 %copy.9 = f32[12,128]{1,0:T(8,128)} copy(f32[12,128]{1,0:T(8,128)S(1)} %get-tuple-element.5) | data formatting | bytes 12288
  (3 shorter events, 0.0 us)
Async XLA Ops:
  0.6 0.7 %copy-start.1 = (s32[128]{0:T(128)S(1)}, s32[128]{0:T(128)}, u32[]{:S(2)}) copy-start(s32[128]{0:T(128)} %param.5) | copy-start | bytes 1540
  0.6 1.6 %copy-start = (bf16[128,1536]{1,0:T(8,128)(2,1)S(1)}, bf16[128,1536]{1,0:T(8,128)(2,1)}, u32[]{:S(2)}) copy-start(bf16[128,1536]{1,0:T(8,128)(2,1)} %q_ref.1) | copy-start | bytes 1179652

commit v5 on v4

--- a/solution.py
+++ b/solution.py
@@ -272,28 +272,34 @@
         keys = jnp.concatenate([kv[lv, y, b, 0:256, :] for lv, y, b in lanes(unit)], 0)
         return lax.dot_general(q, keys, (((1,), (1,)), ((), ())), preferred_element_type=jnp.float32)
 
-    def bias(tile, unit, causal):
+    def documents(unit):
+        rows = [kv[lv, y, b, 256:KS, :].astype(jnp.float32) for lv, y, b in lanes(unit)]
+        return [row[half:half + 1, :] for row in rows for half in range(2)]
+
+    def mask(s, tile, unit, causal):
         xt, h = tile
         own = qseg[xt, h * HALF:(h + 1) * HALF, :]
+        marks = documents(unit)
+        if not causal:
+            own = jnp.concatenate([own] * GROUP, 0)
+            same = jnp.concatenate([own] * len(marks), 1) == jnp.concatenate(marks, 1)
+            return jnp.where(same, s, LOW)
         parts = []
-        for lv, y, b in lanes(unit):
-            rows = kv[lv, y, b, 256:KS, :].astype(jnp.float32)
-            for half in range(2):
-                same = own == rows[half:half + 1, :]
-                if causal:
-                    place = y * 512 + (half * 2 + lane32 // 64) * 128 + b * 64 + lane32 % 64
-                    same = same & (place <= yl * 512 + xt * 128 + c * 64 + h * HALF + row32)
-                parts.append(jnp.where(same, 0.0, LOW))
-        return jnp.concatenate(parts, 1)
+        for i, mark in enumerate(marks):
+            y, b, half = unit[i // 4][1], i // 2 % 2, i % 2
+            place = y * 512 + (half * 2 + lane32 // 64) * 128 + b * 64 + lane32 % 64
+            near = place <= yl * 512 + xt * 128 + c * 64 + h * HALF + row32
+            parts.append(jnp.where((own == mark) & near, 0.0, LOW))
+        return s + jnp.concatenate([jnp.concatenate(parts, 1)] * GROUP, 0)
 
     def absorb(tile, unit, s, causal):
         at = tile[0] * 2 + tile[1]
-        s = s + jnp.concatenate([bias(tile, unit, causal)] * GROUP, 0)
+        s = mask(s, tile, unit, causal)
         before = top[at]
         now = jnp.maximum(before, jnp.max(s, axis=1, keepdims=True))
         top[at] = now
         shrink = jnp.exp2((before - now) * SLOPE)
-        weights = jnp.exp2((s - now[:, :1]) * SLOPE)
+        weights = jnp.exp2((s - jnp.concatenate([now] * 8, 1)) * SLOPE)
         values = jnp.concatenate([kv[lv, y, b, KS:PART, :] for lv, y, b in lanes(unit)], 0)
         values = jnp.concatenate([values, jnp.ones_like(values)], 1)
         sums = jnp.dot(weights.astype(jnp.bfloat16), values, preferred_element_type=jnp.float32)

time: 49.3 us -> 47.7 us (0.968)
  Pallas kernels: 45.5 us -> 44 us
    pallas_call x1, Pallas kernels: 45.5 us -> 44 us  [shards(): pl.pallas_call(kernel, out_shape=(jax.ShapeDtypeStruct((128, 2 * WIDE), b...]
where the time goes in v5:
time: 47.7 us; the launch traced here: 47.6 us
  Pallas kernels  44 us (92%)
  local copies, waits for them, and re-layouts  2.94 us (6%)
  between operations  0.67 us (1%)
    pallas_call x1, Pallas kernels, shards(): pl.pallas_call(kernel, out_shape=(jax.ShapeDtypeStruct((128, 2 * WIDE), b...  44 us
    unnamed x6, local copies, waits for them, and re-layouts  1.99 us

profile of v5, /device:TPU:225, one launch (start us, length us, event | category | flops | bytes accessed | tf_op | source)
XLA Modules:
  0.0 47.6 jit_solution(15885579485112060225)
XLA Ops:
  0.6 0.0 copy-start.1
  0.6 0.0 copy-start
  0.6 0.6 %copy-done.1 = s32[128]{0:T(128)S(1)} copy-done((s32[128]{0:T(128)S(1)}, s32[128]{0:T(128)}, u32[]{:S(2)}) %copy-start.1) | copy-done | bytes 536
  1.3 0.9 %copy.5 = bf16[8,2,32,128]{3,2,1,0:T(8,128)(2,1)S(1)} copy(bf16[8,2,32,128]{3,0,1,2:T(8,128)(2,1)} %bitcast.3) | data formatting | bytes 262144 | tf_op jit(solution)/shard_map/transpose | solution.py:453
  2.3 0.0 copy-done
  2.3 44.0 %shard_map.50 = (bf16[128,1536]{1,0:T(8,128)(2,1)S(1)}, f32[12,128]{1,0:T(8,128)S(1)}) custom-call(bf16[128,1536]{1,0:T(8,128)(2,1)S(1)} %copy-done, bf16[8,80,128]{2,1,0:T(8,128)(2,1)S(1)} %pad_maximum_fusion.pieces), custom_call_target="tpu_custom_call" | custom-call | flops 6000000000 | bytes 1000000 | tf_op jit(solution)/shard_map/pallas_call | solution.py:458
  46.3 0.7 %copy.8 = bf16[128,1536]{1,0:T(8,128)(2,1)} copy(bf16[128,1536]{1,0:T(8,128)(2,1)S(1)} %get-tuple-element.4) | data formatting | bytes 786432
  47.0 0.6 %copy.9 = f32[12,128]{1,0:T(8,128)} copy(f32[12,128]{1,0:T(8,128)S(1)} %get-tuple-element.5) | data formatting | bytes 12288
  (3 shorter events, 0.0 us)
Async XLA Ops:
  0.6 0.7 %copy-start.1 = (s32[128]{0:T(128)S(1)}, s32[128]{0:T(128)}, u32[]{:S(2)}) copy-start(s32[128]{0:T(128)} %param.5) | copy-start | bytes 1540
  0.6 1.6 %copy-start = (bf16[128,1536]{1,0:T(8,128)(2,1)S(1)}, bf16[128,1536]{1,0:T(8,128)(2,1)}, u32[]{:S(2)}) copy-start(bf16[128,1536]{1,0:T(8,128)(2,1)} %q_ref.1) | copy-start | bytes 1179652
